TPU v7x, 32 devices: a whole 2x2x4 slice. The times are simulated.
32 devices in a mesh: pipe: 4 (over y, x), seq: 2 (over core), chan: 4 (over z).
Axes of the slice: x: 2, y: 2, z: 4, core: 2. Of those that a mesh axis runs over, the one named last changes fastest.
Arguments:
- signal: bfloat16 [4, 512, 2048], P('pipe', 'seq', 'chan'), may hold values from -6 to 6
- gate_value: bfloat16 [4, 512, 2048], P('pipe', 'seq', 'chan'), may hold values from -6 to 6
- grad_out: bfloat16 [4, 512, 2048], P('pipe', 'seq', 'chan'), may hold values from -1.5 to 1.5
- long_filter: bfloat16 [4, 512, 2048], P('pipe', 'seq', 'chan'), may hold values from -0.25 to 0.25
- weight: bfloat16 [4, 4096, 2048], P('pipe', None, 'chan'), may hold values from -0.125 to 0.125
Outputs:
- gate_grad: bfloat16 [4, 512, 2048], P('pipe', 'seq', 'chan')
- filter_grad: float32 [4, 512, 2048], P('pipe', 'seq', 'chan')
- input_grad: bfloat16 [4, 512, 4096], P('pipe', 'seq', 'chan')
All inputs are finite; a program needn't handle non-finite values.
Results may differ from a plain program's by a relative error of at most 0.02.
Values may be sent and summed in bfloat16 or wider, within the bound.
A program may use at most 128 MiB of HBM per device.

v0:
```python
import math

import jax
import jax.numpy as jnp
from jax import lax
from jax.sharding import PartitionSpec as P

HIGHEST = lax.Precision.HIGHEST
HIGHER = lax.Precision.HIGH


def passed_along(x, axis, by):
    length = lax.axis_size(axis)
    return lax.ppermute(x, axis, [(i, (i + by) % length) for i in range(length)])


def make_tables(panel_len):
    span_len = 2 * panel_len
    row_index = lax.broadcasted_iota(jnp.int32, (span_len, panel_len), 0)
    col_index = lax.broadcasted_iota(jnp.int32, (span_len, panel_len), 1)
    frequency = jnp.where(row_index <= panel_len, row_index, row_index - panel_len)
    angles = (frequency * col_index % span_len).astype(jnp.float32) * (2.0 * math.pi / span_len)
    forward_table = jnp.where(row_index <= panel_len, jnp.cos(angles), -jnp.sin(angles))
    end_rows = jnp.logical_or(row_index == 0, row_index == panel_len)
    weights = jnp.where(end_rows, 1.0, 2.0) / span_len
    inverse_table = (forward_table * weights).T
    return (forward_table, inverse_table)


def make_parity(panel_len):
    row_index = lax.broadcasted_iota(jnp.int32, (2 * panel_len, 1), 0)
    frequency = jnp.where(row_index <= panel_len, row_index, row_index - panel_len)
    return (1 - 2 * (frequency % 2)).astype(jnp.float32)


def spec_product(left_spec, right_spec, interior, conjugate):
    panel_len = left_spec.shape[0] // 2
    left_real, left_imag = (left_spec[:panel_len], left_spec[panel_len:])
    right_real, right_imag = (right_spec[:panel_len], right_spec[panel_len:])
    if conjugate:
        right_imag = right_imag * (1.0 - 2.0 * interior)
    real_part = left_real * right_real - interior * left_imag * right_imag
    imag_part = (
        interior * (left_real * right_imag + left_imag * right_real)
        + (1.0 - interior) * left_imag * right_imag
    )
    return jnp.concatenate([real_part, imag_part], axis=0)


def on_device(signal, gate_value, grad_out, long_filter, weight):
    panel_len = signal.shape[1]
    chan_width = signal.shape[2]
    span_len = 2 * panel_len
    panel_count = lax.axis_size("seq")
    my_panel = lax.axis_index("seq")
    forward_table, inverse_table = make_tables(panel_len)
    parity = make_parity(panel_len)
    interior = (lax.broadcasted_iota(jnp.int32, (panel_len, 1), 0) != 0).astype(jnp.float32)
    gated = (gate_value[0].astype(jnp.float32) * grad_out[0].astype(jnp.float32)).astype(
        jnp.bfloat16
    )
    signals, gateds, filters = (
        lax.all_gather(signal, "seq", axis=1, tiled=True),
        lax.all_gather(gated[None], "seq", axis=1, tiled=True),
        lax.all_gather(long_filter, "seq", axis=1, tiled=True),
    )
    zero_spec = jnp.zeros((span_len, chan_width), jnp.float32)

    def spectrum(gathered, panel_at):
        panel_rows = lax.dynamic_slice_in_dim(gathered[0], panel_at * panel_len, panel_len, 0)
        return jnp.dot(forward_table, panel_rows.astype(jnp.float32), precision=HIGHER)

    def spectrum_if(use_panel, gathered, panel_at):
        return lax.cond(
            use_panel,
            lambda where_at: spectrum(gathered, where_at),
            lambda where_at: zero_spec,
            panel_at,
        )

    def invert(spectrum_in):
        return jnp.dot(inverse_table, spectrum_in, precision=HIGHEST)

    def settle(lag_parts, spectrum_in, use_panel, target):

        def add_rows(parts_now):
            row_at = jnp.maximum(target, 0)
            current = lax.dynamic_index_in_dim(parts_now, row_at, 0, keepdims=True)
            return lax.dynamic_update_index_in_dim(
                parts_now, current + invert(spectrum_in)[None], row_at, 0
            )

        return lax.cond(use_panel, add_rows, lambda parts_now: parts_now, lag_parts)

    own_gated = jnp.dot(forward_table, gated.astype(jnp.float32), precision=HIGHER)
    last_lag = jnp.maximum(my_panel, panel_count - 1 - my_panel)
    extras = (
        zero_spec,
        jnp.array(False),
        jnp.zeros((panel_count, panel_len, chan_width), jnp.float32),
    )

    def lag_step(lag_index, loop_state):
        prior_filter, forward_sum, backward_sum, extras_now = loop_state
        filter_now = spectrum(filters, lag_index)
        filter_full = filter_now + parity * prior_filter
        use_forward = lag_index <= my_panel
        use_backward = lag_index <= panel_count - 1 - my_panel
        signal_spec = spectrum_if(use_forward, signals, jnp.maximum(my_panel - lag_index, 0))
        gated_spec = spectrum_if(
            use_backward, gateds, jnp.minimum(my_panel + lag_index, panel_count - 1)
        )
        forward_sum = forward_sum + spec_product(filter_full, signal_spec, interior, False)
        backward_sum = backward_sum + spec_product(gated_spec, filter_full, interior, True)
        prior_pair, prior_flag, lag_parts = extras_now
        pair_spec = spec_product(own_gated, signal_spec, interior, True)
        ready = jnp.logical_and(lag_index >= 1, jnp.logical_or(prior_flag, use_forward))
        lag_parts = settle(lag_parts, prior_pair + parity * pair_spec, ready, lag_index - 1)
        extras_now = (pair_spec, use_forward, lag_parts)
        return (filter_now, forward_sum, backward_sum, extras_now)

    unused_filter, forward_sum, backward_sum, extras = lax.fori_loop(
        0, last_lag + 1, lag_step, (zero_spec, zero_spec, zero_spec, extras)
    )
    prior_pair, prior_flag, lag_parts = extras
    lag_parts = settle(lag_parts, prior_pair, prior_flag, last_lag)
    filter_grad = lax.psum_scatter(
        lag_parts.reshape(1, panel_count * panel_len, chan_width).astype(jnp.bfloat16),
        "seq",
        scatter_dimension=1,
        tiled=True,
    ).astype(jnp.float32)
    conv = invert(forward_sum)
    gate_grad = (grad_out[0].astype(jnp.float32) * conv).astype(jnp.bfloat16)[None]
    signal_grad = invert(backward_sum).astype(jnp.bfloat16)
    received = passed_along(signal_grad[None], "pipe", -1)
    partial_sums = lax.dot_general(
        received[0], weight[0], (((1,), (1,)), ((), ())), preferred_element_type=jnp.float32
    )
    input_grad = lax.psum_scatter(
        partial_sums[None], "chan", scatter_dimension=2, tiled=True
    ).astype(jnp.bfloat16)
    return (gate_grad, filter_grad, input_grad)


def solution(mesh):
    return jax.shard_map(
        on_device,
        mesh=mesh,
        in_specs=(
            P("pipe", "seq", "chan"),
            P("pipe", "seq", "chan"),
            P("pipe", "seq", "chan"),
            P("pipe", "seq", "chan"),
            P("pipe", None, "chan"),
        ),
        out_specs=(P("pipe", "seq", "chan"), P("pipe", "seq", "chan"), P("pipe", "seq", "chan")),
        check_vma=False,
    )
```

profile of v0, /device:TPU:0, one launch (start us, length us, event | category | flops | bytes accessed | tf_op | source)
XLA Modules:
  0.0 186.2 jit_solution(11551398261961295438)
XLA Ops:
  7.2 0.0 reduce-scatter.3.cloned.1.call-start
  7.3 1.1 fusion.53
  8.4 4.8 %fusion.62 = f32[512,512]{1,0:T(8,128)} fusion(bf16[1,256,512]{2,1,0:T(8,128)(2,1)} %param.17, bf16[1,256,512]{2,1,0:T(8,128)(2,1)} %param.16, s32[512]{0:T(512)S(1)} %iota_add_fusion, pred[512]{0:T(512)(128)(4,1)S(1)} %iota_compare_fusion.2), kind=kOutput, calls=%fused_computation.100 | convolution fusion | flops 405405696 | bytes 1575424 | tf_op jit(solution)/shard_map/dot_general | solution.py:95
  13.2 1.0 fusion.59
  14.2 2.4 %all_gather.11 = bf16[1,512,512]{2,1,0:T(8,128)(2,1)} all-gather(bf16[1,256,512]{2,1,0:T(8,128)(2,1)S(1)} %fusion.53), channel_id=1, replica_groups=mesh['pipe'=4,'seq'=2,'chan'=4] {'seq'}, dimensions={1}, use_global_device_ids=true | all-gather | bytes 786432 | tf_op jit(solution)/shard_map/all_gather | solution.py:64
  16.6 2.3 %all_gather.10 = bf16[1,512,512]{2,1,0:T(8,128)(2,1)} all-gather(bf16[1,256,512]{2,1,0:T(8,128)(2,1)S(1)} %copy-done.5), channel_id=1, replica_groups=mesh['pipe'=4,'seq'=2,'chan'=4] {'seq'}, dimensions={1}, use_global_device_ids=true | all-gather | bytes 786432 | tf_op jit(solution)/shard_map/all_gather | solution.py:63
  18.9 2.3 %all_gather.9 = bf16[1,512,512]{2,1,0:T(8,128)(2,1)} all-gather(bf16[1,256,512]{2,1,0:T(8,128)(2,1)S(1)} %copy-done.6), channel_id=1, replica_groups=mesh['pipe'=4,'seq'=2,'chan'=4] {'seq'}, dimensions={1}, use_global_device_ids=true | all-gather | bytes 786432 | tf_op jit(solution)/shard_map/all_gather | solution.py:65
  21.2 0.1 broadcast_in_dim.37
  21.3 1.1 broadcast_in_dim.37.clone
  22.5 1.1 broadcast_in_dim.37.clone.1
  23.6 1.1 broadcast_in_dim.37.clone.2
  24.7 1.1 broadcast_in_dim.38
  25.8 45.2 %while.31 = (s32[]{:T(128)}, f32[512,512]{1,0:T(8,128)S(1)}, f32[512,512]{1,0:T(8,128)}, f32[512,512]{1,0:T(8,128)}, f32[512,512]{1,0:T(8,128)}, /*index=5*/pred...) while((s32[]{:T(128)}, f32[512,512]{1,0:T(8,128)S(1)}, ...), condition=%wide.region_7.8_spmd.clone.clone.clone, body=%wide.region_0.7_spmd.clone.clone.clone.sunk | while | flops 2027169536 | bytes 49307344 | solution.py:122
  25.8 4.6 %multiply_add_fusion.5 = (f32[512,512]{1,0:T(8,128)}, f32[512,512]{1,0:T(8,128)S(1)}) fusion(f32[512,512]{1,0:T(8,128)S(1)} %get-tuple-element.810, f32[512]{0:T(512)S(1)} %bitcast.75, s32[512]{0:T(512)S(1)} %get-tuple-element.844, pred[512]{0:T(512)(128)(4,1)S(1)} %get-tuple-element.845, bf16[1,512,512]{2,1,0:T(8,128)(2,1)} %get-tuple-element.838, ...), kind=kOutput, calls=%fused_computation.35.clone.1 | convolution fusion | flops 405405696 | bytes 3412484 | tf_op jit(solution)/shard_map/while/body/dot_general | solution.py:71
  30.4 2.2 %negate_select_fusion.15 = f32[512,256]{1,0:T(8,128)S(1)} fusion(s32[512]{0:T(512)S(1)} %get-tuple-element.844, pred[512]{0:T(512)(128)(4,1)S(1)} %get-tuple-element.845), kind=kLoop, calls=%fused_computation.48.clone.2 | loop fusion | flops 2228224 | bytes 526848 | tf_op jit(solution)/shard_map/jit(_where)/select_n | solution.py:23
  32.7 2.0 %conditional.17 = (f32[256,512]{1,0:T(8,128)S(1)}, f32[256,512]{1,0:T(8,128)S(1)}) conditional(s32[]{:T(128)} %convert_element_type.268, () %tuple.137, (s32[]{:T(128)}, s32[]{:T(128)}, bf16[1,512,512]{2,1,0:T(8,128)(2,1)}, f32[512,256]{1,0:T(8,128)S(1)}) %tuple.138), branch_computations={%region_1.1_spmd, %region_2.2_spmd} | conditional | flops 402653184 | bytes 6029402 | solution.py:74
  32.7 1.5 convolution_bitcast_fusion
  34.2 0.1 fusion.80
  34.3 0.2 copy.39
  34.5 0.2 copy.41
  34.7 2.0 %conditional.18 = (f32[256,512]{1,0:T(8,128)S(1)}, f32[256,512]{1,0:T(8,128)S(1)}) conditional(s32[]{:T(128)} %convert_element_type.269, () %tuple.139, (s32[]{:T(128)}, s32[]{:T(128)}, bf16[1,512,512]{2,1,0:T(8,128)(2,1)}, f32[512,256]{1,0:T(8,128)S(1)}) %tuple.140), branch_computations={%region_3.3_spmd, %region_4.4_spmd} | conditional | flops 402653184 | bytes 6029402 | solution.py:74
  34.7 1.5 convolution_bitcast_fusion.1
  36.2 0.1 fusion.81
  36.3 0.2 copy.43
  36.5 0.2 copy.45
  36.7 0.8 copy-done
  37.5 3.2 %multiply_subtract_fusion.7 = (f32[256,512]{1,0:T(8,128)S(1)}, f32[256,512]{1,0:T(8,128)S(1)}, f32[256,512]{1,0:T(8,128)S(1)}, f32[256,512]{1,0:T(8,128)S(1)}, f32[256,512]{1,0:T(8,128)S(1)}, /*index=5*/f32[256,512]{1,0:T(8,128)}) fusion(f32[256,512]{1,0:T(8,128)S(1)} %get-tuple-element.765, f32[256,512]{1,0:T(8,128)S(1)} %get-tuple-element.766, ...), kind=kLoop, calls=%fused_computation.54.clone.1 | loop fusion | flops 4587520 | bytes 7343104 | tf_op jit(solution)/shard_map/while/body/sub | solution.py:42
  40.6 0.1 pad_maximum_fusion.2
  40.7 0.3 fusion.90
  41.1 1.0 copy.77
  42.0 3.6 %maximum_add_fusion.3 = (f32[512,512]{1,0:T(8,128)}, f32[512,512]{1,0:T(8,128)}) fusion(f32[512,512]{1,0:T(8,128)} %get-tuple-element.811, f32[256,512]{1,0:T(8,128)S(1)} %get-tuple-element.772, f32[256,512]{1,0:T(8,128)S(1)} %get-tuple-element.773, f32[512,512]{1,0:T(8,128)} %get-tuple-element.812, f32[256,512]{1,0:T(8,128)S(1)} %get-tuple-element.774, ...), kind=kLoop, calls=%fused_computation.32.clone.1 | loop fusion | flops 1048576 | bytes 6291456 | tf_op jit(solution)/shard_map/while/body/add | solution.py:113
  45.6 4.6 %multiply_add_fusion.5 = (f32[512,512]{1,0:T(8,128)}, f32[512,512]{1,0:T(8,128)S(1)}) fusion(f32[512,512]{1,0:T(8,128)S(1)} %get-tuple-element.810, f32[512]{0:T(512)S(1)} %bitcast.75, s32[512]{0:T(512)S(1)} %get-tuple-element.844, pred[512]{0:T(512)(128)(4,1)S(1)} %get-tuple-element.845, bf16[1,512,512]{2,1,0:T(8,128)(2,1)} %get-tuple-element.838, ...), kind=kOutput, calls=%fused_computation.35.clone.1 | convolution fusion | flops 405405696 | bytes 3412484 | tf_op jit(solution)/shard_map/while/body/dot_general | solution.py:71
  50.3 2.2 %negate_select_fusion.15 = f32[512,256]{1,0:T(8,128)S(1)} fusion(s32[512]{0:T(512)S(1)} %get-tuple-element.844, pred[512]{0:T(512)(128)(4,1)S(1)} %get-tuple-element.845), kind=kLoop, calls=%fused_computation.48.clone.2 | loop fusion | flops 2228224 | bytes 526848 | tf_op jit(solution)/shard_map/jit(_where)/select_n | solution.py:23
  52.5 0.1 conditional.17
  52.5 0.1 slice.54.clone
  52.6 0.1 slice.54.clone2
  52.7 2.0 %conditional.18 = (f32[256,512]{1,0:T(8,128)S(1)}, f32[256,512]{1,0:T(8,128)S(1)}) conditional(s32[]{:T(128)} %convert_element_type.269, () %tuple.139, (s32[]{:T(128)}, s32[]{:T(128)}, bf16[1,512,512]{2,1,0:T(8,128)(2,1)}, f32[512,256]{1,0:T(8,128)S(1)}) %tuple.140), branch_computations={%region_3.3_spmd, %region_4.4_spmd} | conditional | flops 402653184 | bytes 6029402 | solution.py:74
  52.7 1.5 convolution_bitcast_fusion.1
  54.2 0.1 fusion.81
  54.3 0.2 copy.43
  54.5 0.2 copy.45
  54.7 0.8 copy-done
  55.5 3.2 %multiply_subtract_fusion.7 = (f32[256,512]{1,0:T(8,128)S(1)}, f32[256,512]{1,0:T(8,128)S(1)}, f32[256,512]{1,0:T(8,128)S(1)}, f32[256,512]{1,0:T(8,128)S(1)}, f32[256,512]{1,0:T(8,128)S(1)}, /*index=5*/f32[256,512]{1,0:T(8,128)}) fusion(f32[256,512]{1,0:T(8,128)S(1)} %get-tuple-element.765, f32[256,512]{1,0:T(8,128)S(1)} %get-tuple-element.766, ...), kind=kLoop, calls=%fused_computation.54.clone.1 | loop fusion | flops 4587520 | bytes 7343104 | tf_op jit(solution)/shard_map/while/body/sub | solution.py:42
  58.6 0.1 pad_maximum_fusion.2
  58.7 0.3 fusion.90
  59.0 7.4 %conditional.19 = (f32[2,256,512]{1,2,0:T(8,128)}) conditional(s32[]{:T(128)} %convert_element_type.270, f32[2,256,512]{1,2,0:T(8,128)} %get-tuple-element.815, (s32[]{:T(128)}, f32[2,256,512]{1,2,0:T(8,128)}, f32[512,1]{0,1:T(1,128)S(1)}, f32[512,512]{1,0:T(8,128)S(1)}, f32[512,512]{1,0:T(8,128)}, /*index=5*/pred[256,512]{1,0:T(32,128)(4,1)S(1)}, ...), branch_computations={%region_5.5_spmd, %region_6.6_spmd} | conditional | flops 806354944 | bytes 4329508 | solution.py:93
  59.0 7.4 %fusion.15 = f32[2,256,512]{1,2,0:T(8,128)} fusion(f32[2,256,512]{1,2,0:T(8,128)} %get-tuple-element.335, s32[]{:T(128)S(6)} %max.13, f32[512,512]{1,0:T(8,128)} %get-tuple-element.337, f32[512,512]{1,0:T(8,128)S(1)} %get-tuple-element.339, pred[256,512]{1,0:T(32,128)(4,1)S(1)} %get-tuple-element.572, f32[256,512]{1,0:T(8,128)S(1)} %get-tuple-element.578, ...), kind=kOutput, calls=%fused_computation.14 | convolution fusion | flops 806354944 | bytes 4329476 | tf_op jit(solution)/shard_map/while/body/cond/branch_1_fun/dot_general | solution.py:82
  66.4 1.0 copy.77
  67.4 3.6 %maximum_add_fusion.3 = (f32[512,512]{1,0:T(8,128)}, f32[512,512]{1,0:T(8,128)}) fusion(f32[512,512]{1,0:T(8,128)} %get-tuple-element.811, f32[256,512]{1,0:T(8,128)S(1)} %get-tuple-element.772, f32[256,512]{1,0:T(8,128)S(1)} %get-tuple-element.773, f32[512,512]{1,0:T(8,128)} %get-tuple-element.812, f32[256,512]{1,0:T(8,128)S(1)} %get-tuple-element.774, ...), kind=kLoop, calls=%fused_computation.32.clone.1 | loop fusion | flops 1048576 | bytes 6291456 | tf_op jit(solution)/shard_map/while/body/add | solution.py:113
  71.0 2.7 %conditional.4 = (f32[2,256,512]{2,1,0:T(8,128)}) conditional(s32[]{:T(128)} %convert_element_type.151, (f32[2,256,512]{1,2,0:T(8,128)}) %tuple.103, (s32[]{:T(128)}, f32[2,256,512]{1,2,0:T(8,128)}, pred[256,512]{1,0:T(32,128)(4,1)S(1)}, f32[512,512]{1,0:T(8,128)}, f32[512]{0:T(512)S(1)}, /*index=5*/f32[256,512]{1,0:T(8,128)}, ...), branch_computations={%region_8.9_spmd, %region_9.10_spmd} | conditional | flops 805830656 | bytes 5376024 | solution.py:93
  71.1 2.7 %copy.46 = f32[2,256,512]{2,1,0:T(8,128)} copy(f32[2,256,512]{1,2,0:T(8,128)} %get-tuple-element.580) | data formatting | bytes 2097152 | tf_op jit(solution)/shard_map/while | solution.py:122
  73.7 2.1 %convert_element_type.152 = bf16[2,256,512]{2,1,0:T(8,128)(2,1)} convert(f32[2,256,512]{2,1,0:T(8,128)} %get-tuple-element.851) | non-fusion elementwise | flops 262144 | bytes 1572864 | tf_op jit(solution)/shard_map/convert_element_type | solution.py:128
  75.8 0.0 reduce-scatter.3.cloned.1.call-update
  75.8 0.0 reduce-scatter.5.cloned.1.call-start
  75.9 3.3 %fusion.49 = bf16[1,256,512]{2,1,0:T(8,128)(2,1)S(1)} fusion(f32[512,512]{1,0:T(8,128)S(1)} %copy-done.2, f32[512]{0:T(512)S(1)} %get-tuple-element.864, s32[512]{0:T(512)S(1)} %get-tuple-element.860, pred[512]{0:T(512)(128)(4,1)S(1)} %get-tuple-element.863), kind=kOutput, calls=%fused_computation.77 | convolution fusion | flops 807796736 | bytes 1315328 | tf_op jit(solution)/shard_map/dot_general | solution.py:82
  79.1 3.9 %collective-permute-start = (bf16[1,256,512]{2,1,0:T(8,128)(2,1)S(1)}, bf16[1,256,512]{2,1,0:T(8,128)(2,1)S(1)}, u32[]{:S(2)}, u32[]{:S(2)}) collective-permute-start(bf16[1,256,512]{2,1,0:T(8,128)(2,1)S(1)} %fusion.49), channel_id=1, source_target_pairs={{0,24},{8,0},{16,8},{24,16},{1,25},{9,1},{17,9},{25,17},{2,26},{10... | collective-permute-start | bytes 786440 | tf_op jit(solution)/shard_map/ppermute | solution.py:14
  83.0 3.9 %collective-permute-done = bf16[1,256,512]{2,1,0:T(8,128)(2,1)S(1)} collective-permute-done((bf16[1,256,512]{2,1,0:T(8,128)(2,1)S(1)}, bf16[1,256,512]{2,1,0:T(8,128)(2,1)S(1)}, u32[]{:S(2)}, u32[]{:S(2)}) %collective-permute-start) | collective-permute-done | bytes 262176 | tf_op jit(solution)/shard_map/ppermute | solution.py:14
  86.9 5.4 %convolution_bitcast_fusion.5 = f32[1,256,4096]{2,1,0:T(8,128)} fusion(bf16[1,4096,512]{2,1,0:T(8,128)(2,1)} %param.19, bf16[1,256,512]{2,1,0:T(8,128)(2,1)S(1)} %collective-permute-done), kind=kOutput, calls=%fused_computation.72 | convolution fusion | flops 1073741824 | bytes 8650752 | tf_op jit(solution)/shard_map/dot_general | solution.py:137
  92.3 1.2 copy-done.1
  93.6 0.0 copy-done.7
  93.6 4.0 %fusion.50 = bf16[1,256,512]{2,1,0:T(8,128)(2,1)} fusion(f32[512,512]{1,0:T(8,128)S(1)} %copy-done.1, bf16[1,256,512]{2,1,0:T(8,128)(2,1)S(1)} %copy-done.7, f32[512]{0:T(512)S(1)} %get-tuple-element.864, s32[512]{0:T(512)S(1)} %get-tuple-element.860, pred[512]{0:T(512)(128)(4,1)S(1)} %get-tuple-element.863), kind=kOutput, calls=%fused_computation.78 | convolution fusion | flops 808058880 | bytes 1577472 | tf_op jit(solution)/shard_map/dot_general | solution.py:82
  97.6 1.8 convert_element_type.154
  99.4 77.9 %reduce-scatter.5.cloned.1.call-done = f32[1,256,1024]{2,1,0:T(8,128)} async-done(((f32[1,256,4096]{2,1,0:T(8,128)}), f32[1,256,1024]{2,1,0:T(8,128)}) %reduce-scatter.5.cloned.1.call-update) | async-done | bytes 1048592 | tf_op jit(solution)/shard_map/reduce_scatter | solution.py:140
  177.3 2.1 %convert_element_type.156 = bf16[1,256,1024]{2,1,0:T(8,128)(2,1)} convert(f32[1,256,1024]{2,1,0:T(8,128)} %reduce-scatter.5.cloned.1.call-done) | non-fusion elementwise | flops 262144 | bytes 1572864 | tf_op jit(solution)/shard_map/convert_element_type | solution.py:142
  (33 shorter events, 0.2 us)
Async XLA Ops:
  7.2 9.5 %copy-start.5 = (bf16[1,256,512]{2,1,0:T(8,128)(2,1)S(1)}, bf16[1,256,512]{2,1,0:T(8,128)(2,1)}, u32[]{:S(2)}) copy-start(bf16[1,256,512]{2,1,0:T(8,128)(2,1)} %param.15) | copy-start | bytes 786436
  7.2 11.7 %copy-start.6 = (bf16[1,256,512]{2,1,0:T(8,128)(2,1)S(1)}, bf16[1,256,512]{2,1,0:T(8,128)(2,1)}, u32[]{:S(2)}) copy-start(bf16[1,256,512]{2,1,0:T(8,128)(2,1)} %param.18) | copy-start | bytes 786436
  7.2 90.4 %reduce-scatter.3.cloned.1.call-start = ((), (), s32[]{:S(2)}) async-start(), calls=%async_computation.2 | async-start | bytes 786432 | tf_op jit(solution)/shard_map/reduce_scatter | solution.py:127
  30.4 2.2 %copy-start.3 = (f32[512,512]{1,0:T(8,128)}, f32[512,512]{1,0:T(8,128)S(1)}, u32[]{:S(2)}) copy-start(f32[512,512]{1,0:T(8,128)S(1)} %get-tuple-element.831) | copy-start | bytes 3145732 | tf_op jit(solution)/shard_map/while
  36.7 0.8 copy-start
  42.0 3.6 %copy-start.4 = (f32[512,512]{1,0:T(8,128)S(1)}, f32[512,512]{1,0:T(8,128)}, u32[]{:S(2)}) copy-start(f32[512,512]{1,0:T(8,128)} %copy-done.3) | copy-start | bytes 3145732 | tf_op jit(solution)/shard_map/while
  50.3 2.2 %copy-start.3 = (f32[512,512]{1,0:T(8,128)}, f32[512,512]{1,0:T(8,128)S(1)}, u32[]{:S(2)}) copy-start(f32[512,512]{1,0:T(8,128)S(1)} %get-tuple-element.831) | copy-start | bytes 3145732 | tf_op jit(solution)/shard_map/while
  54.7 0.8 copy-start
  67.4 3.6 %copy-start.4 = (f32[512,512]{1,0:T(8,128)S(1)}, f32[512,512]{1,0:T(8,128)}, u32[]{:S(2)}) copy-start(f32[512,512]{1,0:T(8,128)} %copy-done.3) | copy-start | bytes 3145732 | tf_op jit(solution)/shard_map/while
  71.0 4.8 %copy-start.2 = (f32[512,512]{1,0:T(8,128)S(1)}, f32[512,512]{1,0:T(8,128)}, u32[]{:S(2)}) copy-start(f32[512,512]{1,0:T(8,128)} %get-tuple-element.394) | copy-start | bytes 3145732
  75.8 101.5 %reduce-scatter.5.cloned.1.call-start = ((), (), s32[]{:S(2)}) async-start(), calls=%async_computation.3 | async-start | bytes 5242880 | tf_op jit(solution)/shard_map/reduce_scatter | solution.py:140
  79.1 7.8 %collective-permute-start = (bf16[1,256,512]{2,1,0:T(8,128)(2,1)S(1)}, bf16[1,256,512]{2,1,0:T(8,128)(2,1)S(1)}, u32[]{:S(2)}, u32[]{:S(2)}) collective-permute-start(bf16[1,256,512]{2,1,0:T(8,128)(2,1)S(1)} %fusion.49), channel_id=1, source_target_pairs={{0,24},{8,0},{16,8},{24,16},{1,25},{9,1},{17,9},{25,17},{2,26},{10... | collective-permute-start | bytes 786440 | tf_op jit(solution)/shard_map/ppermute | solution.py:14
  92.3 1.3 copy-start.1
  92.3 1.3 copy-start.7
Sparse Core Ops, SparseCore 0:
  75.9 17.5 reduce-scatter.2
  95.9 81.2 reduce-scatter.4
where the time goes:
time: 187 us; the launch traced here: 186 us
  waiting for transfers between devices  81.8 us (44%)
  matrix products  38.6 us (21%)
  other arithmetic  26.8 us (14%)
  between operations  14.1 us (8%)
  local copies, waits for them, and re-layouts  13.6 us (7%)
  blocking collectives  6.98 us (4%)
  starting transfers between devices  3.94 us (2%)
    reduce_scatter x1, waiting for transfers between devices, on_device(): lax.psum_scatter(partial_sums[None], 'chan', scatter_dimension=2, tiled=T...  77.9 us
    dot_general x3, matrix products, invert(): return jnp.dot(inverse_table, spectrum_in, precision=HIGHEST)  14.6 us
    dot_general x5, matrix products, spectrum(): jnp.dot(forward_table, panel_rows.astype(jnp.float32), precision=HIGHER)  13.7 us
    add x2, other arithmetic, lag_step(): forward_sum + spec_product(filter_full, signal_spec, interior, False)  7.19 us
    sub x2, other arithmetic, spec_product(): real_part = left_real * right_real - interior * left_imag * right_imag  6.34 us
    dot_general x1, matrix products, on_device(): lax.dot_general(received[0], weight[0], (((1,), (1,)), ((), ())), preferr...  5.41 us
    dot_general x1, matrix products, on_device(): jnp.dot(forward_table, gated.astype(jnp.float32), precision=HIGHER)  4.78 us
    select_n x2, other arithmetic, make_tables(): jnp.where(row_index <= panel_len, jnp.cos(angles), -jnp.sin(angles))  4.4 us
  transfers between devices with their start and end apart: 3, of which 2 were waited for; matrix products, arithmetic and copies ran while one was open for 8% of the time, Pallas kernels for 0%

commit v1 on v0

--- a/solution.py
+++ b/solution.py
@@ -1,8 +1,12 @@
+import functools
 import math
 
 import jax
 import jax.numpy as jnp
+import numpy as np
 from jax import lax
+from jax.experimental import pallas as pl
+from jax.experimental.pallas import tpu as pltpu
 from jax.sharding import PartitionSpec as P
 
 HIGHEST = lax.Precision.HIGHEST
@@ -143,9 +147,300 @@
     return (gate_grad, filter_grad, input_grad)
 
 
+MESH = pl.DeviceIdType.MESH
+F32 = jnp.float32
+BF16 = jnp.bfloat16
+CHUNKS = 4
+
+
+def odd_tables(length):
+    steps = np.outer(2 * np.arange(length) + 1, np.arange(length)) % (4 * length)
+    angles = steps * (math.pi / (2 * length))
+    forward = np.concatenate([np.cos(angles), np.sin(angles)], axis=0)
+    return forward.astype(BF16), (forward.T / length).astype(BF16)
+
+
+def dot(a, b):
+    return jnp.dot(a, b, preferred_element_type=F32)
+
+
+def dot_t(a, b):
+    return lax.dot_general(a, b, (((1,), (1,)), ((), ())), preferred_element_type=F32)
+
+
+def relay_order(groups):
+    order = []
+    for i in range((groups + 1) // 2):
+        order += [groups - 1 - i, i]
+    return list(dict.fromkeys(order))
+
+
+def fused_kernel(
+    groups, pipes,
+    signal, gate_value, grad_out, long_filter, weight, table, inverse,
+    gate_grad, filter_grad, input_grad,
+    table_v, inverse_v, weight_v, filter_v, signal_v, gated_v, gate_v, grad_v,
+    filter_spec, gated_spec, signal_spec, product, sent_v, received_v,
+    parts, from_left, from_right, going, gate_grad_v, filter_grad_v, input_grad_v,
+    local_sem, seq_send, seq_recv, pipe_send, pipe_recv, going_sem, left_sem, right_sem, out_sem,
+):
+    rows, width = gate_v.shape
+    freqs = table_v.shape[0] // 2
+    chunk = rows // CHUNKS
+    outs = going.shape[3]
+    me_pipe, me_seq, me = lax.axis_index("pipe"), lax.axis_index("seq"), lax.axis_index("chan")
+    before = lax.rem(me_pipe + pipes - 1, pipes)
+    after = lax.rem(me_pipe + 1, pipes)
+    partner = 1 - me_seq
+    last = groups - 1
+
+    barrier = pltpu.get_barrier_semaphore()
+    greeted = [{"seq": partner}, {"pipe": before}, {"pipe": after}]
+    greeted += [{"chan": lax.rem(me + 1, groups)}, {"chan": lax.rem(me + groups - 1, groups)}]
+    for device in greeted:
+        pl.semaphore_signal(barrier, inc=1, device_id=device, device_id_type=MESH)
+
+    own = pl.ds(pl.multiple_of(me_seq * rows, rows), rows)
+
+    loads = {}
+    for i, (name, src, dst) in enumerate([
+        ("gate", gate_value.at[0], gate_v),
+        ("grad", grad_out.at[0], grad_v),
+        ("filter", long_filter.at[0], filter_v.at[own]),
+        ("table", table, table_v),
+        ("inverse", inverse.at[own], inverse_v),
+        ("signal", signal.at[0], signal_v.at[own]),
+        ("weight", weight.at[0], weight_v),
+    ]):
+        loads[name] = pltpu.make_async_copy(src, dst, local_sem.at[i])
+        loads[name].start()
+
+    def to_partner(at, src, dst):
+        return pltpu.make_async_remote_copy(
+            src_ref=src, dst_ref=dst, send_sem=seq_send.at[at], recv_sem=seq_recv.at[at],
+            device_id={"seq": partner}, device_id_type=MESH,
+        )
+
+    filter_copy = to_partner(0, long_filter.at[0], filter_v.at[own])
+    gated_copy = to_partner(1, gated_v.at[own], gated_v.at[own])
+    signal_copy = to_partner(2, signal.at[0], signal_v.at[own])
+    pl.semaphore_wait(barrier, len(greeted))
+    filter_copy.start()
+    loads["gate"].wait()
+    loads["grad"].wait()
+    gated_v[own, :] = (gate_v[...].astype(F32) * grad_v[...].astype(F32)).astype(BF16)
+    gated_copy.start()
+    signal_copy.start()
+
+    tile = min(256, width)
+    tiles = [
+        (pl.ds(f, tile), pl.ds(freqs + f, tile), pl.ds(c, tile))
+        for c in range(0, width, tile)
+        for f in range(0, freqs, tile)
+    ]
+    loads["table"].wait()
+    loads["filter"].wait()
+    filter_copy.wait_recv()
+    for re, im, ch in tiles:
+        filter_spec[re, ch] = dot(table_v[re, :], filter_v[:, ch])
+        filter_spec[im, ch] = dot(table_v[im, :], filter_v[:, ch])
+    gated_copy.wait_recv()
+    for re, im, ch in tiles:
+        g_re, g_im = dot(table_v[re, :], gated_v[:, ch]), dot(table_v[im, :], gated_v[:, ch])
+        h_re, h_im = filter_spec[re, ch], filter_spec[im, ch]
+        gated_spec[re, ch] = g_re
+        gated_spec[im, ch] = g_im
+        product[re, ch] = (h_re * g_re + h_im * g_im).astype(BF16)
+        product[im, ch] = (h_re * g_im - h_im * g_re).astype(BF16)
+    loads["inverse"].wait()
+
+    def piece(r):
+        return pl.ds(r * chunk, chunk)
+
+    passed = [
+        pltpu.make_async_remote_copy(
+            src_ref=sent_v.at[piece(r)], dst_ref=received_v.at[piece(r)],
+            send_sem=pipe_send.at[r], recv_sem=pipe_recv.at[r],
+            device_id={"pipe": before}, device_id_type=MESH,
+        )
+        for r in range(CHUNKS)
+    ]
+    half = rows // 2
+    for h in range(2):
+        at = pl.ds(h * half, half)
+        sent_v[at, :] = dot(inverse_v[at, :], product[...]).astype(BF16)
+        for r in range(h * CHUNKS // 2, (h + 1) * CHUNKS // 2):
+            passed[r].start()
+
+    loads["signal"].wait()
+    signal_copy.wait_recv()
+
+    def convolve():
+        for re, im, ch in tiles:
+            s_re, s_im = dot(table_v[re, :], signal_v[:, ch]), dot(table_v[im, :], signal_v[:, ch])
+            h_re, h_im = filter_spec[re, ch], filter_spec[im, ch]
+            signal_spec[re, ch] = s_re
+            signal_spec[im, ch] = s_im
+            product[re, ch] = (h_re * s_re - h_im * s_im).astype(BF16)
+            product[im, ch] = (h_re * s_im + h_im * s_re).astype(BF16)
+        conv = dot(inverse_v[...], product[...])
+        gate_grad_v[...] = (grad_v[...].astype(F32) * conv).astype(BF16)
+        gate_grad_out.start()
+
+    def correlate():
+        for re, im, ch in tiles:
+            s_re, s_im = signal_spec[re, ch], signal_spec[im, ch]
+            g_re, g_im = gated_spec[re, ch], gated_spec[im, ch]
+            product[re, ch] = (s_re * g_re + s_im * g_im).astype(BF16)
+            product[im, ch] = (s_re * g_im - s_im * g_re).astype(BF16)
+        filter_grad_v[...] = dot(inverse_v[...], product[...])
+        filter_grad_out.start()
+
+    gate_grad_out = pltpu.make_async_copy(gate_grad_v, gate_grad.at[0], out_sem.at[0])
+    filter_grad_out = pltpu.make_async_copy(filter_grad_v, filter_grad.at[0], out_sem.at[1])
+    input_grad_out = [
+        pltpu.make_async_copy(
+            input_grad_v.at[piece(r)], input_grad.at[0, piece(r)], out_sem.at[2 + r]
+        )
+        for r in range(CHUNKS)
+    ]
+
+    def rightward(r, d):
+        return pltpu.make_async_remote_copy(
+            src_ref=going.at[r, d], dst_ref=from_left.at[r, d],
+            send_sem=going_sem.at[r, d], recv_sem=left_sem.at[r, d],
+            device_id={"chan": lax.rem(me + 1, groups)}, device_id_type=MESH,
+        )
+
+    def leftward(r, d):
+        return pltpu.make_async_remote_copy(
+            src_ref=going.at[r, d], dst_ref=from_right.at[r, d],
+            send_sem=going_sem.at[r, d], recv_sem=right_sem.at[r, d],
+            device_id={"chan": lax.rem(me + groups - 1, groups)}, device_id_type=MESH,
+        )
+
+    def multiply(r):
+        passed[r].wait_recv()
+        block = received_v[piece(r), :]
+        for j in range(groups):
+            d = jnp.where(2 * me < groups, last - j, j)
+            at = pl.ds(pl.multiple_of(d * outs, outs), outs)
+            parts[r, d] = dot_t(block, weight_v[at, :])
+
+            @pl.when(jnp.logical_and(me == 0, d > 0))
+            def _():
+                going[r, d] = parts[r, d].astype(BF16)
+                rightward(r, d).start()
+
+            @pl.when(jnp.logical_and(me == last, d < last))
+            def _():
+                going[r, d] = parts[r, d].astype(BF16)
+                leftward(r, d).start()
+
+    def relay(r):
+        for d in relay_order(groups):
+            @pl.when(jnp.logical_and(me > 0, me < d))
+            def _():
+                rightward(r, d).wait_recv()
+                going[r, d] = (parts[r, d] + from_left[r, d].astype(F32)).astype(BF16)
+                rightward(r, d).start()
+
+            @pl.when(jnp.logical_and(me < last, me > d))
+            def _():
+                leftward(r, d).wait_recv()
+                going[r, d] = (parts[r, d] + from_right[r, d].astype(F32)).astype(BF16)
+                leftward(r, d).start()
+
+    def finish(r):
+        @pl.when(me > 0)
+        def _():
+            rightward(r, me).wait_recv()
+            parts[r, me] = parts[r, me] + from_left[r, me].astype(F32)
+
+        @pl.when(me < last)
+        def _():
+            leftward(r, me).wait_recv()
+            parts[r, me] = parts[r, me] + from_right[r, me].astype(F32)
+
+        input_grad_v[piece(r), :] = parts[r, me].astype(BF16)
+        input_grad_out[r].start()
+
+    convolve()
+    loads["weight"].wait()
+    for r in range(CHUNKS):
+        multiply(r)
+        if r == 1:
+            correlate()
+        if r > 0:
+            relay(r - 1)
+    finish(0)
+    relay(CHUNKS - 1)
+    for r in range(1, CHUNKS):
+        finish(r)
+
+    for copy in (filter_copy, gated_copy, signal_copy, *passed):
+        copy.wait_send()
+    for r in range(CHUNKS):
+        for d in range(groups):
+            @pl.when(me != d)
+            def _():
+                rightward(r, d).wait_send()
+    gate_grad_out.wait()
+    filter_grad_out.wait()
+    for copy in input_grad_out:
+        copy.wait()
+
+
+def fused(signal, gate_value, grad_out, long_filter, weight):
+    groups, pipes = lax.axis_size("chan"), lax.axis_size("pipe")
+    _, rows, width = signal.shape
+    length = 2 * rows
+    model = weight.shape[1]
+    outs, chunk = model // groups, rows // CHUNKS
+    forward, inverse = odd_tables(length)
+    moved = pltpu.VMEM((CHUNKS, groups, chunk, outs), BF16)
+    spec = pltpu.VMEM((2 * length, width), F32)
+    panel = pltpu.VMEM((rows, width), BF16)
+    whole = pltpu.VMEM((length, width), BF16)
+    sems = pltpu.SemaphoreType.DMA
+    anywhere = pl.BlockSpec(memory_space=pl.ANY)
+    macs = 6 * 2 * length * length * width + rows * width * model
+    return pl.pallas_call(
+        functools.partial(fused_kernel, groups, pipes),
+        out_shape=(
+            jax.ShapeDtypeStruct((1, rows, width), BF16),
+            jax.ShapeDtypeStruct((1, rows, width), F32),
+            jax.ShapeDtypeStruct((1, rows, outs), BF16),
+        ),
+        in_specs=[anywhere] * 7,
+        out_specs=(anywhere,) * 3,
+        scratch_shapes=[
+            pltpu.VMEM((2 * length, length), BF16),
+            pltpu.VMEM((rows, 2 * length), BF16),
+            pltpu.VMEM((model, width), BF16),
+            whole, whole, whole, panel, panel,
+            spec, spec, spec,
+            pltpu.VMEM((2 * length, width), BF16),
+            panel, panel,
+            pltpu.VMEM((CHUNKS, groups, chunk, outs), F32),
+            moved, moved, moved,
+            panel,
+            pltpu.VMEM((rows, width), F32),
+            pltpu.VMEM((rows, outs), BF16),
+            sems((7,)), sems((3,)), sems((3,)), sems((CHUNKS,)), sems((CHUNKS,)),
+            sems((CHUNKS, groups)), sems((CHUNKS, groups)), sems((CHUNKS, groups)),
+            sems((2 + CHUNKS,)),
+        ],
+        compiler_params=pltpu.CompilerParams(
+            collective_id=0, has_side_effects=True, vmem_limit_bytes=48 * 1024 * 1024
+        ),
+        cost_estimate=pl.CostEstimate(flops=2 * macs, bytes_accessed=2 * model * width, transcendentals=0),
+    )(signal, gate_value, grad_out, long_filter, weight, jnp.asarray(forward), jnp.asarray(inverse))
+
+
 def solution(mesh):
     return jax.shard_map(
-        on_device,
+        fused if mesh.shape["seq"] == 2 else on_device,
         mesh=mesh,
         in_specs=(
             P("pipe", "seq", "chan"),

time: 187 us -> 71 us (0.38)
  waiting for transfers between devices: 81.8 us -> 0 us
  Pallas kernels: 0 us -> 61.5 us
  matrix products: 38.6 us -> 0 us
  other arithmetic: 26.8 us -> 0 us
  between operations: 14.1 us -> 0.65 us
  blocking collectives: 6.98 us -> 0 us
  local copies, waits for them, and re-layouts: 13.6 us -> 8.53 us
  starting transfers between devices: 3.94 us -> 0 us
    reduce_scatter x2 -> x0, waiting for transfers between devices: 77.9 us -> none  [the longest x1 77.9 us: on_device(): lax.psum_scatter(partial_sums[None], 'chan', scatter_dimension=2, tiled=T...]
    pallas_call x0 -> x1, Pallas kernels: none -> 61.5 us  [fused(): pl.pallas_call(functools.partial(fused_kernel, groups, pipes), out_shape=...]
    dot_general x10 -> x0, matrix products: 38.6 us -> none  [the longest x3 14.6 us: invert(): return jnp.dot(inverse_table, spectrum_in, precision=HIGHEST)]
    unnamed x10 -> x15, local copies, waits for them, and re-layouts: 1.29 us -> 8.53 us
    add x2 -> x0, other arithmetic: 7.19 us -> none  [lag_step(): forward_sum + spec_product(filter_full, signal_spec, interior, False)]
    convert_element_type x8 -> x0, other arithmetic: 7.16 us -> none  [the longest x1 2.09 us: on_device(): input_grad = lax.psum_scatter(partial_sums[None], 'chan', scatter_dimensi...]
    all_gather x3 -> x0, blocking collectives: 6.98 us -> none  [the longest x1 2.38 us: on_device(): lax.all_gather(gated[None], 'seq', axis=1, tiled=True)]
    sub x5 -> x0, other arithmetic: 6.35 us -> none  [the longest x2 6.34 us: spec_product(): real_part = left_real * right_real - interior * left_imag * right_imag]
  transfers between devices with their start and end apart: 3 -> 0, of which waited for: 2 -> 0; matrix products, arithmetic and copies ran while one was open for 8% -> 0% of each run, Pallas kernels for 0% -> 0%
where the time goes in v1:
time: 71 us; the launch traced here: 70.6 us
  Pallas kernels  61.5 us (87%)
  local copies, waits for them, and re-layouts  8.53 us (12%)
    pallas_call x1, Pallas kernels, fused(): pl.pallas_call(functools.partial(fused_kernel, groups, pipes), out_shape=...  61.5 us
    unnamed x15, local copies, waits for them, and re-layouts  8.53 us

profile of v1, /device:TPU:0, one launch (start us, length us, event | category | flops | bytes accessed | tf_op | source)
XLA Modules:
  0.0 70.6 jit_solution(3269817528903542367)
XLA Ops:
  0.6 0.0 copy-start
  0.6 0.9 %copy-done = bf16[1,256,512]{2,1,0:T(8,128)(2,1)S(1)} copy-done((bf16[1,256,512]{2,1,0:T(8,128)(2,1)S(1)}, bf16[1,256,512]{2,1,0:T(8,128)(2,1)}, u32[]{:S(2)}) %copy-start) | copy-done | bytes 262168
  1.6 0.0 copy-start.1
  1.6 0.9 %copy-done.1 = bf16[1,256,512]{2,1,0:T(8,128)(2,1)S(1)} copy-done((bf16[1,256,512]{2,1,0:T(8,128)(2,1)S(1)}, bf16[1,256,512]{2,1,0:T(8,128)(2,1)}, u32[]{:S(2)}) %copy-start.1) | copy-done | bytes 262168
  2.5 0.0 copy-start.2
  2.5 0.9 %copy-done.2 = bf16[1,256,512]{2,1,0:T(8,128)(2,1)S(1)} copy-done((bf16[1,256,512]{2,1,0:T(8,128)(2,1)S(1)}, bf16[1,256,512]{2,1,0:T(8,128)(2,1)}, u32[]{:S(2)}) %copy-start.2) | copy-done | bytes 262168
  3.5 0.0 copy-start.3
  3.5 0.9 %copy-done.3 = bf16[1,256,512]{2,1,0:T(8,128)(2,1)S(1)} copy-done((bf16[1,256,512]{2,1,0:T(8,128)(2,1)S(1)}, bf16[1,256,512]{2,1,0:T(8,128)(2,1)}, u32[]{:S(2)}) %copy-start.3) | copy-done | bytes 262168
  4.4 0.0 copy-start.4
  4.4 1.2 %copy-done.4 = bf16[512,1024]{1,0:T(8,128)(2,1)S(1)} copy-done((bf16[512,1024]{1,0:T(8,128)(2,1)S(1)}, bf16[512,1024]{1,0:T(8,128)(2,1)}, u32[]{:S(2)}) %copy-start.4) | copy-done | bytes 1048600
  5.7 0.0 copy-start.5
  5.7 1.2 %copy-done.5 = bf16[1024,512]{1,0:T(8,128)(2,1)S(1)} copy-done((bf16[1024,512]{1,0:T(8,128)(2,1)S(1)}, bf16[1024,512]{1,0:T(8,128)(2,1)}, u32[]{:S(2)}) %copy-start.5) | copy-done | bytes 1048600
  6.9 61.5 %shard_map.94 = (bf16[1,256,512]{2,1,0:T(8,128)(2,1)S(1)}, f32[1,256,512]{2,1,0:T(8,128)S(1)}, bf16[1,256,1024]{2,1,0:T(8,128)(2,1)S(1)}) custom-call(bf16[1,256,512]{2,1,0:T(8,128)(2,1)S(1)} %copy-done, bf16[1,256,512]{2,1,0:T(8,128)(2,1)S(1)} %copy-done.1, bf16[1,256,512]{2,1,0:T(8,128)(2,1)S(1)} %copy-done.2, bf16[1,256,512]{2,1,0:T(8,128)(2,1)S(1)} %copy-done.3, ...), custom_call_target="tpu_custom_call" | custom-call | flops 4294967296 | bytes 4194304 | tf_op jit(solution)/shard_map/pallas_call | solution.py:408
  68.4 0.7 copy.13
  69.1 0.8 %copy.14 = f32[1,256,512]{2,1,0:T(8,128)} copy(f32[1,256,512]{2,1,0:T(8,128)S(1)} %get-tuple-element.7) | data formatting | bytes 1048576
  69.9 0.8 %copy.15 = bf16[1,256,1024]{2,1,0:T(8,128)(2,1)} copy(bf16[1,256,1024]{2,1,0:T(8,128)(2,1)S(1)} %get-tuple-element.8) | data formatting | bytes 1048576
Async XLA Ops:
  0.6 1.0 %copy-start = (bf16[1,256,512]{2,1,0:T(8,128)(2,1)S(1)}, bf16[1,256,512]{2,1,0:T(8,128)(2,1)}, u32[]{:S(2)}) copy-start(bf16[1,256,512]{2,1,0:T(8,128)(2,1)} %signal.1) | copy-start | bytes 786436
  1.6 0.9 %copy-start.1 = (bf16[1,256,512]{2,1,0:T(8,128)(2,1)S(1)}, bf16[1,256,512]{2,1,0:T(8,128)(2,1)}, u32[]{:S(2)}) copy-start(bf16[1,256,512]{2,1,0:T(8,128)(2,1)} %gate_value.1) | copy-start | bytes 786436
  2.5 0.9 %copy-start.2 = (bf16[1,256,512]{2,1,0:T(8,128)(2,1)S(1)}, bf16[1,256,512]{2,1,0:T(8,128)(2,1)}, u32[]{:S(2)}) copy-start(bf16[1,256,512]{2,1,0:T(8,128)(2,1)} %grad_out.1) | copy-start | bytes 786436
  3.5 0.9 %copy-start.3 = (bf16[1,256,512]{2,1,0:T(8,128)(2,1)S(1)}, bf16[1,256,512]{2,1,0:T(8,128)(2,1)}, u32[]{:S(2)}) copy-start(bf16[1,256,512]{2,1,0:T(8,128)(2,1)} %long_filter.1) | copy-start | bytes 786436
  4.4 1.2 %copy-start.4 = (bf16[512,1024]{1,0:T(8,128)(2,1)S(1)}, bf16[512,1024]{1,0:T(8,128)(2,1)}, u32[]{:S(2)}) copy-start(bf16[512,1024]{1,0:T(8,128)(2,1)} %constant.5.clone.inverse) | copy-start | bytes 3145732
  5.7 1.2 %copy-start.5 = (bf16[1024,512]{1,0:T(8,128)(2,1)S(1)}, bf16[1024,512]{1,0:T(8,128)(2,1)}, u32[]{:S(2)}) copy-start(bf16[1024,512]{1,0:T(8,128)(2,1)} %constant.4.clone.table) | copy-start | bytes 3145732

commit v2 on v1

--- a/solution.py
+++ b/solution.py
@@ -151,6 +151,7 @@
 F32 = jnp.float32
 BF16 = jnp.bfloat16
 CHUNKS = 4
+VMEM_BYTES = 62 * 1024 * 1024
 
 
 def odd_tables(length):
@@ -275,7 +276,7 @@
     loads["signal"].wait()
     signal_copy.wait_recv()
 
-    def convolve():
+    def convolve_start():
         for re, im, ch in tiles:
             s_re, s_im = dot(table_v[re, :], signal_v[:, ch]), dot(table_v[im, :], signal_v[:, ch])
             h_re, h_im = filter_spec[re, ch], filter_spec[im, ch]
@@ -283,6 +284,8 @@
             signal_spec[im, ch] = s_im
             product[re, ch] = (h_re * s_re - h_im * s_im).astype(BF16)
             product[im, ch] = (h_re * s_im + h_im * s_re).astype(BF16)
+
+    def convolve_end():
         conv = dot(inverse_v[...], product[...])
         gate_grad_v[...] = (grad_v[...].astype(F32) * conv).astype(BF16)
         gate_grad_out.start()
@@ -365,11 +368,12 @@
         input_grad_v[piece(r), :] = parts[r, me].astype(BF16)
         input_grad_out[r].start()
 
-    convolve()
+    convolve_start()
     loads["weight"].wait()
     for r in range(CHUNKS):
         multiply(r)
         if r == 1:
+            convolve_end()
             correlate()
         if r > 0:
             relay(r - 1)
@@ -389,6 +393,28 @@
     filter_grad_out.wait()
     for copy in input_grad_out:
         copy.wait()
+
+
+def settle_kernel(*refs):
+    count = (len(refs) - 1) // 2
+    sources, targets, sems = refs[:count], refs[count : 2 * count], refs[-1]
+    copies = [pltpu.make_async_copy(sources[i], targets[i], sems.at[i]) for i in range(count)]
+    for copy in copies:
+        copy.start()
+    for copy in copies:
+        copy.wait()
+
+
+def settled(arrays):
+    anywhere = pl.BlockSpec(memory_space=pl.ANY)
+    return pl.pallas_call(
+        settle_kernel,
+        out_shape=tuple(jax.ShapeDtypeStruct(x.shape, x.dtype) for x in arrays),
+        in_specs=[anywhere] * len(arrays),
+        out_specs=(anywhere,) * len(arrays),
+        scratch_shapes=[pltpu.SemaphoreType.DMA((len(arrays),))],
+        compiler_params=pltpu.CompilerParams(vmem_limit_bytes=VMEM_BYTES),
+    )(*arrays)
 
 
 def fused(signal, gate_value, grad_out, long_filter, weight):
@@ -405,7 +431,7 @@
     sems = pltpu.SemaphoreType.DMA
     anywhere = pl.BlockSpec(memory_space=pl.ANY)
     macs = 6 * 2 * length * length * width + rows * width * model
-    return pl.pallas_call(
+    grads = pl.pallas_call(
         functools.partial(fused_kernel, groups, pipes),
         out_shape=(
             jax.ShapeDtypeStruct((1, rows, width), BF16),
@@ -432,10 +458,11 @@
             sems((2 + CHUNKS,)),
         ],
         compiler_params=pltpu.CompilerParams(
-            collective_id=0, has_side_effects=True, vmem_limit_bytes=48 * 1024 * 1024
+            collective_id=0, has_side_effects=True, vmem_limit_bytes=VMEM_BYTES
         ),
         cost_estimate=pl.CostEstimate(flops=2 * macs, bytes_accessed=2 * model * width, transcendentals=0),
     )(signal, gate_value, grad_out, long_filter, weight, jnp.asarray(forward), jnp.asarray(inverse))
+    return settled(grads)
 
 
 def solution(mesh):

time: 71 us -> 104 us (1.46)
  Pallas kernels: 61.5 us -> 103 us
  local copies, waits for them, and re-layouts: 8.53 us -> 0 us
    pallas_call x0 -> x1, Pallas kernels: none -> 40.8 us  [settled(): pl.pallas_call(settle_kernel, out_shape=tuple((jax.ShapeDtypeStruct(x.sha...]
    unnamed x15 -> x0, local copies, waits for them, and re-layouts: 8.53 us -> none
where the time goes in v2:
time: 104 us
  Pallas kernels  103 us (99%)
    pallas_call x1, Pallas kernels, fused(): pl.pallas_call(functools.partial(fused_kernel, groups, pipes), out_shape=...  62.2 us
    pallas_call x1, Pallas kernels, settled(): pl.pallas_call(settle_kernel, out_shape=tuple((jax.ShapeDtypeStruct(x.sha...  40.8 us

profile of v2, /device:TPU:0, one launch (start us, length us, event | category | flops | bytes accessed | tf_op | source)
XLA Modules:
  0.0 103.7 jit_solution(8613653553843175378)
XLA Ops:
  0.6 62.2 %shard_map.94 = (bf16[1,256,512]{2,1,0:T(8,128)(2,1)}, f32[1,256,512]{2,1,0:T(8,128)}, bf16[1,256,1024]{2,1,0:T(8,128)(2,1)}) custom-call(bf16[1,256,512]{2,1,0:T(8,128)(2,1)} %signal.1, bf16[1,256,512]{2,1,0:T(8,128)(2,1)} %gate_value.1, bf16[1,256,512]{2,1,0:T(8,128)(2,1)} %grad_out.1, bf16[1,256,512]{2,1,0:T(8,128)(2,1)} %long_filter.1, ...), custom_call_target="tpu_custom_call" | custom-call | flops 4294967296 | bytes 4194304 | tf_op jit(solution)/shard_map/pallas_call | solution.py:434
  62.8 40.8 %shard_map.95 = (bf16[1,256,512]{2,1,0:T(8,128)(2,1)}, f32[1,256,512]{2,1,0:T(8,128)}, bf16[1,256,1024]{2,1,0:T(8,128)(2,1)}) custom-call(bf16[1,256,512]{2,1,0:T(8,128)(2,1)} %get-tuple-element.6.refs_0_, f32[1,256,512]{2,1,0:T(8,128)} %get-tuple-element.7.refs_1_, bf16[1,256,1024]{2,1,0:T(8,128)(2,1)} %get-tuple-element.8.refs_2_), custom_call_target="tpu_custom_call" | custom-call | tf_op jit(solution)/shard_map/pallas_call | solution.py:410

commit v3 on v1

--- a/solution.py
+++ b/solution.py
@@ -151,6 +151,7 @@
 F32 = jnp.float32
 BF16 = jnp.bfloat16
 CHUNKS = 4
+VMEM_BYTES = 62 * 1024 * 1024
 
 
 def odd_tables(length):
@@ -275,7 +276,7 @@
     loads["signal"].wait()
     signal_copy.wait_recv()
 
-    def convolve():
+    def convolve_start():
         for re, im, ch in tiles:
             s_re, s_im = dot(table_v[re, :], signal_v[:, ch]), dot(table_v[im, :], signal_v[:, ch])
             h_re, h_im = filter_spec[re, ch], filter_spec[im, ch]
@@ -283,6 +284,8 @@
             signal_spec[im, ch] = s_im
             product[re, ch] = (h_re * s_re - h_im * s_im).astype(BF16)
             product[im, ch] = (h_re * s_im + h_im * s_re).astype(BF16)
+
+    def convolve_end():
         conv = dot(inverse_v[...], product[...])
         gate_grad_v[...] = (grad_v[...].astype(F32) * conv).astype(BF16)
         gate_grad_out.start()
@@ -365,11 +368,12 @@
         input_grad_v[piece(r), :] = parts[r, me].astype(BF16)
         input_grad_out[r].start()
 
-    convolve()
+    convolve_start()
     loads["weight"].wait()
     for r in range(CHUNKS):
         multiply(r)
         if r == 1:
+            convolve_end()
             correlate()
         if r > 0:
             relay(r - 1)
@@ -432,7 +436,7 @@
             sems((2 + CHUNKS,)),
         ],
         compiler_params=pltpu.CompilerParams(
-            collective_id=0, has_side_effects=True, vmem_limit_bytes=48 * 1024 * 1024
+            collective_id=0, has_side_effects=True, vmem_limit_bytes=VMEM_BYTES
         ),
         cost_estimate=pl.CostEstimate(flops=2 * macs, bytes_accessed=2 * model * width, transcendentals=0),
     )(signal, gate_value, grad_out, long_filter, weight, jnp.asarray(forward), jnp.asarray(inverse))

time: 71 us -> 68.5 us (0.965)
  local copies, waits for them, and re-layouts: 8.53 us -> 5.4 us
    unnamed x15 -> x3, local copies, waits for them, and re-layouts: 8.53 us -> 5.4 us
    pallas_call x1, Pallas kernels: 61.5 us -> 62.2 us  [fused(): pl.pallas_call(functools.partial(fused_kernel, groups, pipes), out_shape=...]
where the time goes in v3:
time: 68.5 us; the launch traced here: 68.2 us
  Pallas kernels  62.2 us (91%)
  local copies, waits for them, and re-layouts  5.4 us (8%)
    pallas_call x1, Pallas kernels, fused(): pl.pallas_call(functools.partial(fused_kernel, groups, pipes), out_shape=...  62.2 us
    unnamed x3, local copies, waits for them, and re-layouts  5.4 us

profile of v3, /device:TPU:0, one launch (start us, length us, event | category | flops | bytes accessed | tf_op | source)
XLA Modules:
  0.0 68.2 jit_solution(221986294150461932)
XLA Ops:
  0.6 62.2 %shard_map.94 = (bf16[1,256,512]{2,1,0:T(8,128)(2,1)}, f32[1,256,512]{2,1,0:T(8,128)}, bf16[1,256,1024]{2,1,0:T(8,128)(2,1)}) custom-call(bf16[1,256,512]{2,1,0:T(8,128)(2,1)} %signal.1, bf16[1,256,512]{2,1,0:T(8,128)(2,1)} %gate_value.1, bf16[1,256,512]{2,1,0:T(8,128)(2,1)} %grad_out.1, bf16[1,256,512]{2,1,0:T(8,128)(2,1)} %long_filter.1, ...), custom_call_target="tpu_custom_call" | custom-call | flops 4294967296 | bytes 4194304 | tf_op jit(solution)/shard_map/pallas_call | solution.py:412
  62.8 1.7 %copy.13 = bf16[1,256,512]{2,1,0:T(8,128)(2,1)} copy(bf16[1,256,512]{2,1,0:T(8,128)(2,1)} %get-tuple-element.6) | data formatting | bytes 524288
  64.5 1.9 %copy.14 = f32[1,256,512]{2,1,0:T(8,128)} copy(f32[1,256,512]{2,1,0:T(8,128)} %get-tuple-element.7) | data formatting | bytes 1048576
  66.4 1.9 %copy.15 = bf16[1,256,1024]{2,1,0:T(8,128)(2,1)} copy(bf16[1,256,1024]{2,1,0:T(8,128)(2,1)} %get-tuple-element.8) | data formatting | bytes 1048576
